TPU v7x, 32 devices: a whole 2x2x4 slice. The times are simulated.
32 devices in a mesh: tgt: 4 (over y, x), inner: 8 (over z, core).
Axes of the slice: x: 2, y: 2, z: 4, core: 2. Of those that a mesh axis runs over, the one named last changes fastest.
Arguments:
- near_tiles: bfloat16 [128, 1024, 1024], P(('tgt', 'inner')), may hold values from -0.1875 to 0.1875
- near_target: int32 [128], P(('tgt', 'inner')), may hold values from 0 to 7
- near_right: int32 [128], P(('tgt', 'inner')), may hold values from 0 to 31
- near_count: int32 [32], P(('tgt', 'inner')), may hold values from 1 to 4, as said below
- low_u: bfloat16 [1024, 64, 1024], P(('tgt', 'inner')), may hold values from -0.75 to 0.75
- low_v: bfloat16 [1024, 64, 1024], P(('tgt', 'inner')), may hold values from -0.1875 to 0.1875
- low_target: int32 [1024], P(('tgt', 'inner')), may hold values from 0 to 7, as said below
- low_right: int32 [1024], P(('tgt', 'inner')), may hold values from 0 to 31
- right_u: bfloat16 [256, 64, 1024], P(('tgt', 'inner')), may hold values from -6 to 6
- right_v: bfloat16 [256, 64, 1024], P(('tgt', 'inner')), may hold values from -0.25 to 0.25
- probe_seed: int32 [32], P('tgt'), may hold values from 1 to 29999
Outputs:
- basis_out: float32 [32, 64, 1024], P('tgt', None, 'inner')
- image_out: float32 [32, 64, 1024], P('tgt', None, 'inner')
Inputs may be any that keep to these rules, and one draw needn't show every extreme that they name: `near_count`: some device holds 4 live slots. `low_target`: the 32 low-rank pairs of each device name every target tile of its group.
All inputs are finite; a program needn't handle non-finite values.
Results may differ from a plain program's by a relative error of at most 0.004.
Values may be sent and summed in bfloat16 or wider, within the bound.
A program may use at most 128 MiB of HBM per device.

v0:
```python
import functools
import math

import jax
import jax.numpy as jnp
from jax import lax
from jax.experimental import pallas as pl
from jax.experimental.pallas import tpu as pltpu
from jax.sharding import PartitionSpec as P

HIGHEST = lax.Precision.HIGHEST
MESH = pl.DeviceIdType.MESH
F32 = jnp.float32
BF16 = jnp.bfloat16
VMEM_LIMIT = 56 * 1024 * 1024


def nt_dot(a, b):
    return lax.dot_general(a, b, (((1,), (1,)), ((), ())), preferred_element_type=F32)


def nn_dot(a, b):
    return lax.dot_general(a, b, (((1,), (0,)), ((), ())), preferred_element_type=F32)


def split(x):
    hi = x.astype(BF16)
    return hi, (x - hi.astype(F32)).astype(BF16)


def probe_table(seeds, rank_size, order):
    shape = (seeds.shape[0], rank_size, order)
    chan = lax.broadcasted_iota(jnp.int32, shape, 1)
    place = lax.broadcasted_iota(jnp.int32, shape, 2)
    code = (
        seeds[:, None, None] * 9973
        + place * place * 7
        + place * chan * 131
        + chan * chan * 17
        + place * 7919
        + chan * 104729
    ) % 65521
    return ((code.astype(F32) - 32760.0) / 32768.0).astype(BF16)


def gather_kernel(nt, u_ref, v_ref, su_ref, sv_ref, send, recv, local):
    me = lax.axis_index("tgt")
    k = u_ref.shape[0]
    mine = pl.ds(me * k, k)
    lu = pltpu.make_async_copy(u_ref, su_ref.at[mine], local.at[0])
    lv = pltpu.make_async_copy(v_ref, sv_ref.at[mine], local.at[1])
    lu.start()
    lv.start()
    barrier = pltpu.get_barrier_semaphore()

    def push(src, dst, sem, to):
        copy = pltpu.make_async_remote_copy(
            src_ref=src,
            dst_ref=dst,
            send_sem=send.at[sem],
            recv_sem=recv.at[sem],
            device_id={"tgt": to},
            device_id_type=MESH,
        )
        copy.start()
        return copy

    copies = []
    if nt == 4:
        a = me + 1 - 2 * (me % 2)
        b = (me + 2) % 4
        for peer in (a, b):
            pl.semaphore_signal(barrier, inc=1, device_id={"tgt": peer}, device_id_type=MESH)
        pl.semaphore_wait(barrier, 2)
        ua = push(u_ref, su_ref.at[mine], 0, a)
        vb = push(v_ref, sv_ref.at[mine], 1, b)
        va = push(v_ref, sv_ref.at[mine], 2, a)
        ub = push(u_ref, su_ref.at[mine], 3, b)
        from_a = pl.ds(a * k, k)
        from_b = pl.ds(b * k, k)
        ua.wait_recv()
        fu = push(su_ref.at[from_a], su_ref.at[from_a], 4, b)
        vb.wait_recv()
        fv = push(sv_ref.at[from_b], sv_ref.at[from_b], 5, a)
        for c in (va, ub, fu, fv):
            c.wait_recv()
        copies = [ua, vb, va, ub, fu, fv]
    else:
        for d in range(1, nt):
            pl.semaphore_signal(
                barrier, inc=1, device_id={"tgt": (me + d) % nt}, device_id_type=MESH
            )
        pl.semaphore_wait(barrier, nt - 1)
        for d in range(1, nt):
            to = (me + d) % nt
            copies.append(push(u_ref, su_ref.at[mine], 2 * d - 2, to))
            copies.append(push(v_ref, sv_ref.at[mine], 2 * d - 1, to))
        for c in copies:
            c.wait_recv()
    for c in copies:
        c.wait_send()
    lu.wait()
    lv.wait()


def gather_tiles(nt, u, v):
    sems = 6 if nt == 4 else max(2 * nt - 2, 1)
    shape = jax.ShapeDtypeStruct((nt * u.shape[0],) + u.shape[1:], u.dtype)
    return pl.pallas_call(
        functools.partial(gather_kernel, nt),
        out_shape=(shape, shape),
        in_specs=[pl.BlockSpec(memory_space=pl.ANY)] * 2,
        out_specs=[pl.BlockSpec(memory_space=pl.ANY)] * 2,
        scratch_shapes=[
            pltpu.SemaphoreType.DMA((sems,)),
            pltpu.SemaphoreType.DMA((sems,)),
            pltpu.SemaphoreType.DMA((2,)),
        ],
        compiler_params=pltpu.CompilerParams(collective_id=0, has_side_effects=True),
    )(u, v)


def reduce_kernel(n, gather, x_ref, *refs):
    if gather:
        out_ref, half, part, total, send, recv = refs
    else:
        out_ref, half, part, got_unused, send, recv = refs
    me = lax.axis_index("inner")
    m = n // 2
    z = me // 2
    core = me % 2
    other = 1 - core
    sib = z * 2 + other
    barrier = pltpu.get_barrier_semaphore()
    pl.semaphore_signal(barrier, inc=1, device_id={"inner": sib}, device_id_type=MESH)
    for d in range(1, m):
        peer = ((z + d) % m) * 2 + core
        pl.semaphore_signal(barrier, inc=1, device_id={"inner": peer}, device_id_type=MESH)
    pl.semaphore_wait(barrier, m)

    def push(src, dst, sem, to):
        copy = pltpu.make_async_remote_copy(
            src_ref=src,
            dst_ref=dst,
            send_sem=send.at[sem],
            recv_sem=recv.at[sem],
            device_id={"inner": to},
            device_id_type=MESH,
        )
        copy.start()
        return copy

    pairs = []
    for d in range(m):
        q = (z + 1 + d) % m
        pairs.append(push(x_ref.at[q, other], half.at[q], d, sib))
    sends = []
    for d in range(m):
        q = (z + 1 + d) % m
        pairs[d].wait_recv()
        half[q] = half[q] + x_ref[q, core]
        if d < m - 1:
            sends.append(push(half.at[q], part.at[m - 2 - d], m + d, q * 2 + core))
    acc = half[z]
    for d in range(m - 1):
        sends[d].wait_recv()
        acc = acc + part[m - 2 - d]
    if gather:
        total[...] = acc
        out_ref[z, core] = acc
        outs = [push(total, out_ref.at[z, core], 2 * m - 1, sib)]
        away = []
        for d in range(m - 1):
            q = (z + 1 + d) % m
            away.append(push(total, out_ref.at[z, core], 2 * m + d, q * 2 + core))
        for d in range(m - 1):
            q = (z + 2 * m - 1 - d) % m
            away[d].wait_recv()
            outs.append(push(out_ref.at[q, core], out_ref.at[q, core], 3 * m - 1 + d, sib))
        for c in outs:
            c.wait_recv()
        sends = sends + outs + away
    else:
        out_ref[...] = acc
    for c in pairs + sends:
        c.wait_send()


def reduce_inner(n, x, gather):
    m = n // 2
    block = x.shape[2:]
    sems = 4 * m - 2 if gather else 2 * m - 1
    return pl.pallas_call(
        functools.partial(reduce_kernel, n, gather),
        out_shape=jax.ShapeDtypeStruct(x.shape if gather else block, F32),
        in_specs=[pl.BlockSpec(memory_space=pltpu.VMEM)],
        out_specs=pl.BlockSpec(memory_space=pltpu.VMEM),
        scratch_shapes=[
            pltpu.VMEM((m,) + block, F32),
            pltpu.VMEM((max(m - 1, 1),) + block, F32),
            pltpu.VMEM(block, F32),
            pltpu.SemaphoreType.DMA((sems,)),
            pltpu.SemaphoreType.DMA((sems,)),
        ],
        compiler_params=pltpu.CompilerParams(
            collective_id=1 if gather else 2, has_side_effects=True, vmem_limit_bytes=VMEM_LIMIT
        ),
    )(x)


def near_sketch_kernel(right, target, count, near_ref, u_ref, v_ref, probe_ref, lh_ref, ll_ref, sk_ref):
    j = pl.program_id(0)

    @pl.when(j == 0)
    def _():
        sk_ref[...] = jnp.zeros_like(sk_ref)

    t = target[j]
    live = (j < count[0]).astype(F32)
    left = nt_dot(u_ref[0], near_ref[0]) * live
    lh, ll = split(left)
    lh_ref[0] = lh
    ll_ref[0] = ll
    zh, zl = split(nt_dot(probe_ref[t], v_ref[0]))
    sk_ref[t] += nn_dot(zh, lh) + nn_dot(zl, lh) + nn_dot(zh, ll)


def low_sketch_kernel(batch, right, target, *refs):
    u_refs, v_refs = refs[:batch], refs[batch : 2 * batch]
    low_u_ref, low_v_ref, probe_ref, base_ref, mix_ref, sk_ref = refs[2 * batch :]
    j = pl.program_id(0)

    @pl.when(j == 0)
    def _():
        sk_ref[...] = base_ref[...]

    terms = []
    for o in range(batch):
        t = target[j * batch + o]
        mixing = nt_dot(low_v_ref[o], u_refs[o][0]).astype(BF16)
        mix_ref[o] = mixing
        zh, zl = split(nt_dot(probe_ref[t], v_refs[o][0]))
        qh, ql = split(nt_dot(zh, mixing) + nt_dot(zl, mixing))
        low_u = low_u_ref[o]
        terms.append((t, nn_dot(qh, low_u) + nn_dot(ql, low_u)))
    for t, y in terms:
        sk_ref[t] += y


def add_columns(im_ref, t, y):
    n, share = im_ref.shape[0], im_ref.shape[3]
    for p in range(n):
        im_ref[p, t] += y[:, p * share : (p + 1) * share]


def near_image_kernel(right, target, lh_ref, ll_ref, v_ref, sh_ref, sl_ref, im_ref):
    j = pl.program_id(0)

    @pl.when(j == 0)
    def _():
        im_ref[...] = jnp.zeros_like(im_ref)

    t = target[j]
    sh = sh_ref[t]
    lh = lh_ref[0]
    ph, pll = split(nt_dot(sh, lh) + nt_dot(sl_ref[t], lh) + nt_dot(sh, ll_ref[0]))
    v = v_ref[0]
    add_columns(im_ref, t, nn_dot(ph, v) + nn_dot(pll, v))


def low_image_kernel(batch, right, target, *refs):
    v_refs = refs[:batch]
    low_u_ref, mix_ref, sh_ref, sl_ref, base_ref, im_ref = refs[batch:]
    j = pl.program_id(0)

    @pl.when(j == 0)
    def _():
        im_ref[...] = base_ref[...]

    terms = []
    for o in range(batch):
        t = target[j * batch + o]
        low_u = low_u_ref[o]
        wh, wl = split(nt_dot(sh_ref[t], low_u) + nt_dot(sl_ref[t], low_u))
        mixing = mix_ref[o]
        ph, pll = split(nn_dot(wh, mixing) + nn_dot(wl, mixing))
        v = v_refs[o][0]
        terms.append((t, nn_dot(ph, v) + nn_dot(pll, v)))
    for t, y in terms:
        add_columns(im_ref, t, y)


def chol_inv_kernel(s_ref, out_ref, a_ref):
    tiles, r, _ = s_ref.shape
    row = lax.broadcasted_iota(jnp.int32, (r, r), 0)
    col = lax.broadcasted_iota(jnp.int32, (r, r), 1)
    eye = (row == col).astype(F32)
    for t in range(tiles):
        s = s_ref[t]
        a_ref[t, :, :r] = lax.dot_general(
            s, s, (((1,), (1,)), ((), ())), precision=HIGHEST, preferred_element_type=F32
        )
        a_ref[t, :, r:] = eye
    rows = [a_ref[:, 8 * b : 8 * b + 8, :] for b in range(r // 8)]
    sub = lax.broadcasted_iota(jnp.int32, (tiles, 8, 2 * r), 1)
    for k in range(r):
        b0, e = k // 8, k % 8
        pivot = rows[b0][:, e : e + 1, :]
        inv = 1.0 / pivot[:, :, k : k + 1]
        scaled = pivot * inv
        for b in range(b0, r // 8):
            step = rows[b][:, :, k : k + 1] * scaled
            if b == b0:
                step = jnp.where(sub > e, step, 0.0)
            rows[b] = rows[b] - step
    lane = lax.broadcasted_iota(jnp.int32, (tiles, 8, 2 * r), 2)
    for b in range(r // 8):
        diag = jnp.sum(jnp.where(lane == sub + 8 * b, rows[b], 0.0), axis=2, keepdims=True)
        out_ref[:, 8 * b : 8 * b + 8, :] = (rows[b] * lax.rsqrt(diag))[:, :, r:]


def whole(shape):
    zeros = (0,) * len(shape)
    return pl.BlockSpec(shape, lambda j, *s: zeros)


def at_right(shape, batch, o):
    return pl.BlockSpec((1,) + shape[1:], lambda j, right, *s: (right[j * batch + o], 0, 0))


def per_step(batch, shape):
    return pl.BlockSpec((batch,) + shape[1:], lambda j, *s: (j,) + (0,) * (len(shape) - 1))


def run(kernel, scalars, steps, ins, specs, outs, out_specs):
    return pl.pallas_call(
        kernel,
        grid_spec=pltpu.PrefetchScalarGridSpec(
            num_scalar_prefetch=len(scalars), grid=(steps,), in_specs=specs, out_specs=out_specs
        ),
        out_shape=outs,
        compiler_params=pltpu.CompilerParams(vmem_limit_bytes=VMEM_LIMIT),
    )(*scalars, *ins)


def per_device(
    nt,
    ni,
    near_tiles,
    near_target,
    near_right,
    near_count,
    low_u,
    low_v,
    low_target,
    low_right,
    right_u,
    right_v,
    probe_seed,
):
    slots, order = near_tiles.shape[0], near_tiles.shape[1]
    lows, r = low_u.shape[0], low_u.shape[1]
    tiles = probe_seed.shape[0]
    share = order // ni
    batch = math.gcd(lows, 4)
    seg_u, seg_v = gather_tiles(nt, right_u, right_v)
    probe = probe_table(probe_seed, r, order)
    sk = jax.ShapeDtypeStruct((tiles, r, order), F32)
    left = jax.ShapeDtypeStruct((slots, r, order), BF16)
    lh, ll, near_sk = run(
        near_sketch_kernel,
        (near_right, near_target, near_count),
        slots,
        (near_tiles, seg_u, seg_v, probe),
        [
            per_step(1, near_tiles.shape),
            at_right(seg_u.shape, 1, 0),
            at_right(seg_v.shape, 1, 0),
            whole(probe.shape),
        ],
        (left, left, sk),
        (per_step(1, left.shape), per_step(1, left.shape), whole(sk.shape)),
    )
    mix_shape = jax.ShapeDtypeStruct((lows, r, r), BF16)
    mixing, sketch = run(
        functools.partial(low_sketch_kernel, batch),
        (low_right, low_target),
        lows // batch,
        (seg_u,) * batch + (seg_v,) * batch + (low_u, low_v, probe, near_sk),
        [at_right(seg_u.shape, batch, o) for o in range(batch)] * 2
        + [per_step(batch, low_u.shape), per_step(batch, low_v.shape)]
        + [whole(probe.shape), whole(sk.shape)],
        (mix_shape, sk),
        (per_step(batch, mix_shape.shape), whole(sk.shape)),
    )
    rows = tiles * r // ni
    total = reduce_inner(ni, sketch.reshape(ni // 2, 2, rows, order), True)
    total = total.reshape(tiles, r, order)
    sh, sl = split(total)
    im = jax.ShapeDtypeStruct((ni, tiles, r, share), F32)
    near_im = run(
        near_image_kernel,
        (near_right, near_target),
        slots,
        (lh, ll, seg_v, sh, sl),
        [
            per_step(1, lh.shape),
            per_step(1, ll.shape),
            at_right(seg_v.shape, 1, 0),
            whole(sh.shape),
            whole(sl.shape),
        ],
        im,
        whole(im.shape),
    )
    image = run(
        functools.partial(low_image_kernel, batch),
        (low_right, low_target),
        lows // batch,
        (seg_v,) * batch + (low_u, mixing, sh, sl, near_im),
        [at_right(seg_v.shape, batch, o) for o in range(batch)]
        + [per_step(batch, low_u.shape), per_step(batch, mixing.shape)]
        + [whole(sh.shape), whole(sl.shape), whole(im.shape)],
        im,
        whole(im.shape),
    )
    inverse = pl.pallas_call(
        chol_inv_kernel,
        out_shape=jax.ShapeDtypeStruct((tiles, r, r), F32),
        scratch_shapes=[pltpu.VMEM((tiles, r, 2 * r), F32)],
        compiler_params=pltpu.CompilerParams(vmem_limit_bytes=VMEM_LIMIT),
    )(total)
    summed = reduce_inner(ni, image.reshape(ni // 2, 2, tiles * r, share), False)
    summed = summed.reshape(tiles, r, share)
    mine = lax.dynamic_slice_in_dim(total, lax.axis_index("inner") * share, share, 2)
    basis = jnp.einsum("tde,tei->tdi", inverse, mine, precision=HIGHEST)
    image_out = jnp.einsum("tde,tei->tdi", inverse, summed, precision=HIGHEST)
    return (basis * math.sqrt(order), image_out)


def solution(mesh):
    return jax.shard_map(
        functools.partial(per_device, mesh.shape["tgt"], mesh.shape["inner"]),
        mesh=mesh,
        in_specs=(
            P(("tgt", "inner"), None, None),
            P(("tgt", "inner")),
            P(("tgt", "inner")),
            P(("tgt", "inner")),
            P(("tgt", "inner"), None, None),
            P(("tgt", "inner"), None, None),
            P(("tgt", "inner")),
            P(("tgt", "inner")),
            P(("tgt", "inner"), None, None),
            P(("tgt", "inner"), None, None),
            P("tgt"),
        ),
        out_specs=(P("tgt", None, "inner"), P("tgt", None, "inner")),
        check_vma=False,
    )
```

profile of v0, /device:TPU:9, one launch (start us, length us, event | category | flops | bytes accessed | tf_op | source)
XLA Modules:
  0.0 237.5 jit_solution(9017602772184326971)
XLA Ops:
  0.7 0.7 broadcast_multiply_fusion
  1.3 2.6 %fusion.3.probe_ref.refs_10_ = bf16[8,64,1024]{2,1,0:T(8,128)(2,1)} fusion(s32[64]{0:T(128)S(1)} %get-tuple-element.18, s32[1024]{0:T(1024)S(1)} %get-tuple-element.16, s32[64]{0:T(128)S(1)} %get-tuple-element.19, s32[1024]{0:T(1024)S(1)} %get-tuple-element.17, s32[8]{0:T(128)S(1)} %broadcast_multiply_fusion), kind=kLoop, calls=%fused_computation.4 | loop fusion | flops 8912896 | bytes 1057312 | tf_op jit(solution)/shard_map/convert_element_type | solution.py:43
  3.9 70.4 %shard_map.122 = (bf16[32,64,1024]{2,1,0:T(8,128)(2,1)}, bf16[32,64,1024]{2,1,0:T(8,128)(2,1)}) custom-call(bf16[8,64,1024]{2,1,0:T(8,128)(2,1)} %u_ref.1, bf16[8,64,1024]{2,1,0:T(8,128)(2,1)} %v_ref.1), custom_call_target="tpu_custom_call" | custom-call | tf_op jit(solution)/shard_map/pallas_call | solution.py:109
  75.0 9.6 %shard_map.123 = (bf16[4,64,1024]{2,1,0:T(8,128)(2,1)}, bf16[4,64,1024]{2,1,0:T(8,128)(2,1)}, f32[8,64,1024]{2,1,0:T(8,128)}) custom-call(s32[4]{0:T(128)} %right.6, s32[4]{0:T(128)} %target.6, s32[1]{0:T(128)S(6)} %copy.13.count, bf16[4,1024,1024]{2,1,0:T(8,128)(2,1)} %near_ref.1, ...), custom_call_target="tpu_custom_call" | custom-call | tf_op jit(solution)/shard_map/pallas_call | solution.py:336
  84.6 21.0 %shard_map.124 = (bf16[32,64,64]{2,1,0:T(8,128)(2,1)}, f32[8,64,1024]{2,1,0:T(8,128)}) custom-call(s32[32]{0:T(128)} %right.7, s32[32]{0:T(128)} %target.7, bf16[32,64,1024]{2,1,0:T(8,128)(2,1)} %get-tuple-element.9.u_ref.refs_0_.refs_1_.refs_2_.refs_3_, bf16[32,64,1024]{2,1,0:T(8,128)(2,1)} %get-tuple-element.9.u_ref.refs_0_.refs_1_.refs_2_.refs_3_, ...), custom_call_target="tpu_custom_call" | custom-call | tf_op jit(solution)/shard_map/pallas_call | solution.py:336
  105.6 55.5 %shard_map.125 = f32[4,2,64,1024]{3,2,1,0:T(8,128)} custom-call(f32[4,2,64,1024]{3,2,1,0:T(8,128)} %bitcast.14), custom_call_target="tpu_custom_call" | custom-call | tf_op jit(solution)/shard_map/pallas_call | solution.py:193
  161.1 0.0 copy-start
  161.1 2.9 %bitcast_convert_fusion.sh_ref.refs_6_ = bf16[8,64,1024]{2,1,0:T(8,128)(2,1)} fusion(f32[4,2,64,1024]{3,2,1,0:T(8,128)} %shard_map.125), kind=kLoop, calls=%fused_computation.18 | loop fusion | flops 524288 | bytes 3145728 | tf_op jit(solution)/shard_map/convert_element_type | solution.py:27
  164.0 0.0 copy-done
  164.0 1.2 subtract_convert_fusion.sl_ref.refs_7_
  165.1 6.7 %shard_map.127.refs_8_ = f32[8,8,64,128]{3,2,1,0:T(8,128)} custom-call(s32[4]{0:T(128)} %right.6, s32[4]{0:T(128)} %target.6, bf16[4,64,1024]{2,1,0:T(8,128)(2,1)} %get-tuple-element.14.lh_ref, bf16[4,64,1024]{2,1,0:T(8,128)(2,1)} %get-tuple-element.15.ll_ref, ...), custom_call_target="tpu_custom_call" | custom-call | tf_op jit(solution)/shard_map/pallas_call | solution.py:336
  171.9 18.4 %shard_map.128 = f32[8,8,64,128]{3,2,1,0:T(8,128)} custom-call(s32[32]{0:T(128)} %right.7, s32[32]{0:T(128)} %target.7, bf16[32,64,1024]{2,1,0:T(8,128)(2,1)} %get-tuple-element.10.v_ref.refs_4_.refs_5_.refs_6_.refs_7_.refs_0_.refs_1_.refs_2_.refs_3_, ...), custom_call_target="tpu_custom_call" | custom-call | tf_op jit(solution)/shard_map/pallas_call | solution.py:336
  190.2 32.0 %shard_map.129 = f32[512,128]{1,0:T(8,128)} custom-call(f32[4,2,512,128]{3,2,1,0:T(8,128)} %bitcast.13), custom_call_target="tpu_custom_call" | custom-call | tf_op jit(solution)/shard_map/pallas_call | solution.py:193
  222.3 0.0 copy-start.1
  222.3 11.1 %shard_map.126 = f32[8,64,64]{2,1,0:T(8,128)} custom-call(f32[8,64,1024]{2,1,0:T(8,128)} %bitcast.11), custom_call_target="tpu_custom_call" | custom-call | tf_op jit(solution)/shard_map/pallas_call | solution.py:427
  233.4 0.0 copy-done.1
  233.4 2.0 fusion.9
  235.4 2.1 convolution_multiply_fusion
  (2 shorter events, 0.0 us)
Async XLA Ops:
  161.1 2.9 %copy-start = (f32[4,2,64,1024]{3,2,1,0:T(8,128)S(1)}, f32[4,2,64,1024]{3,2,1,0:T(8,128)}, u32[]{:S(2)}) copy-start(f32[4,2,64,1024]{3,2,1,0:T(8,128)} %shard_map.125) | copy-start | bytes 6291460
  222.3 11.1 %copy-start.1 = (f32[512,128]{1,0:T(8,128)S(1)}, f32[512,128]{1,0:T(8,128)}, u32[]{:S(2)}) copy-start(f32[512,128]{1,0:T(8,128)} %shard_map.129) | copy-start | bytes 786436
where the time goes:
time: 238 us
  Pallas kernels  225 us (95%)
  other arithmetic  7.3 us (3%)
  matrix products  4.15 us (2%)
    pallas_call x2, Pallas kernels, reduce_inner(): pl.pallas_call(functools.partial(reduce_kernel, n, gather), out_shape=jax...  87.5 us
    pallas_call x1, Pallas kernels, gather_tiles(): pl.pallas_call(functools.partial(gather_kernel, nt), out_shape=(shape, sh...  70.4 us
    pallas_call x4, Pallas kernels, run(): pl.pallas_call(kernel, grid_spec=pltpu.PrefetchScalarGridSpec(num_scalar_...  55.8 us
    pallas_call x1, Pallas kernels, per_device(): pl.pallas_call(chol_inv_kernel, out_shape=jax.ShapeDtypeStruct((tiles, r,...  11.1 us

commit v1 on v0

--- a/solution.py
+++ b/solution.py
@@ -122,9 +122,9 @@
 
 def reduce_kernel(n, gather, x_ref, *refs):
     if gather:
-        out_ref, half, part, total, send, recv = refs
+        out_ref, half, cut, part, total, send, recv = refs
     else:
-        out_ref, half, part, got_unused, send, recv = refs
+        out_ref, half, cut, part, send, recv = refs
     me = lax.axis_index("inner")
     m = n // 2
     z = me // 2
@@ -158,16 +158,16 @@
     for d in range(m):
         q = (z + 1 + d) % m
         pairs[d].wait_recv()
-        half[q] = half[q] + x_ref[q, core]
         if d < m - 1:
-            sends.append(push(half.at[q], part.at[m - 2 - d], m + d, q * 2 + core))
-    acc = half[z]
+            cut[d] = (half[q] + x_ref[q, core]).astype(BF16)
+            sends.append(push(cut.at[d], part.at[m - 2 - d], m + d, q * 2 + core))
+    acc = half[z] + x_ref[z, core]
     for d in range(m - 1):
         sends[d].wait_recv()
-        acc = acc + part[m - 2 - d]
+        acc = acc + part[m - 2 - d].astype(F32)
     if gather:
-        total[...] = acc
-        out_ref[z, core] = acc
+        total[...] = acc.astype(BF16)
+        out_ref[z, core] = acc.astype(BF16)
         outs = [push(total, out_ref.at[z, core], 2 * m - 1, sib)]
         away = []
         for d in range(m - 1):
@@ -192,47 +192,31 @@
     sems = 4 * m - 2 if gather else 2 * m - 1
     return pl.pallas_call(
         functools.partial(reduce_kernel, n, gather),
-        out_shape=jax.ShapeDtypeStruct(x.shape if gather else block, F32),
+        out_shape=jax.ShapeDtypeStruct(x.shape, BF16) if gather else jax.ShapeDtypeStruct(block, F32),
         in_specs=[pl.BlockSpec(memory_space=pltpu.VMEM)],
         out_specs=pl.BlockSpec(memory_space=pltpu.VMEM),
         scratch_shapes=[
             pltpu.VMEM((m,) + block, F32),
-            pltpu.VMEM((max(m - 1, 1),) + block, F32),
-            pltpu.VMEM(block, F32),
-            pltpu.SemaphoreType.DMA((sems,)),
-            pltpu.SemaphoreType.DMA((sems,)),
-        ],
+            pltpu.VMEM((max(m - 1, 1),) + block, BF16),
+            pltpu.VMEM((max(m - 1, 1),) + block, BF16),
+        ]
+        + ([pltpu.VMEM(block, BF16)] if gather else [])
+        + [pltpu.SemaphoreType.DMA((sems,)), pltpu.SemaphoreType.DMA((sems,))],
         compiler_params=pltpu.CompilerParams(
             collective_id=1 if gather else 2, has_side_effects=True, vmem_limit_bytes=VMEM_LIMIT
         ),
     )(x)
 
 
-def near_sketch_kernel(right, target, count, near_ref, u_ref, v_ref, probe_ref, lh_ref, ll_ref, sk_ref):
+def sketch_kernel(batch, slots, right, target, near_right, near_target, count, *refs):
+    u_refs, v_refs = refs[:batch], refs[batch : 2 * batch]
+    low_u_ref, low_v_ref, near_ref, nu_ref, nv_ref, probe_ref = refs[2 * batch : 2 * batch + 6]
+    mix_ref, lh_ref, ll_ref, sk_ref = refs[2 * batch + 6 :]
     j = pl.program_id(0)
 
     @pl.when(j == 0)
     def _():
         sk_ref[...] = jnp.zeros_like(sk_ref)
-
-    t = target[j]
-    live = (j < count[0]).astype(F32)
-    left = nt_dot(u_ref[0], near_ref[0]) * live
-    lh, ll = split(left)
-    lh_ref[0] = lh
-    ll_ref[0] = ll
-    zh, zl = split(nt_dot(probe_ref[t], v_ref[0]))
-    sk_ref[t] += nn_dot(zh, lh) + nn_dot(zl, lh) + nn_dot(zh, ll)
-
-
-def low_sketch_kernel(batch, right, target, *refs):
-    u_refs, v_refs = refs[:batch], refs[batch : 2 * batch]
-    low_u_ref, low_v_ref, probe_ref, base_ref, mix_ref, sk_ref = refs[2 * batch :]
-    j = pl.program_id(0)
-
-    @pl.when(j == 0)
-    def _():
-        sk_ref[...] = base_ref[...]
 
     terms = []
     for o in range(batch):
@@ -246,6 +230,17 @@
     for t, y in terms:
         sk_ref[t] += y
 
+    @pl.when(j < slots)
+    def _():
+        t = near_target[j]
+        live = (j < count[0]).astype(F32)
+        left = nt_dot(nu_ref[0], near_ref[0]) * live
+        lh, ll = split(left)
+        lh_ref[0] = lh
+        ll_ref[0] = ll
+        zh, zl = split(nt_dot(probe_ref[t], nv_ref[0]))
+        sk_ref[t] += nn_dot(zh, lh) + nn_dot(zl, lh) + nn_dot(zh, ll)
+
 
 def add_columns(im_ref, t, y):
     n, share = im_ref.shape[0], im_ref.shape[3]
@@ -253,41 +248,33 @@
         im_ref[p, t] += y[:, p * share : (p + 1) * share]
 
 
-def near_image_kernel(right, target, lh_ref, ll_ref, v_ref, sh_ref, sl_ref, im_ref):
+def image_kernel(batch, slots, right, target, near_right, near_target, *refs):
+    v_refs = refs[:batch]
+    low_u_ref, mix_ref, lh_ref, ll_ref, nv_ref, sk_ref, im_ref = refs[batch:]
     j = pl.program_id(0)
 
     @pl.when(j == 0)
     def _():
         im_ref[...] = jnp.zeros_like(im_ref)
 
-    t = target[j]
-    sh = sh_ref[t]
-    lh = lh_ref[0]
-    ph, pll = split(nt_dot(sh, lh) + nt_dot(sl_ref[t], lh) + nt_dot(sh, ll_ref[0]))
-    v = v_ref[0]
-    add_columns(im_ref, t, nn_dot(ph, v) + nn_dot(pll, v))
-
-
-def low_image_kernel(batch, right, target, *refs):
-    v_refs = refs[:batch]
-    low_u_ref, mix_ref, sh_ref, sl_ref, base_ref, im_ref = refs[batch:]
-    j = pl.program_id(0)
-
-    @pl.when(j == 0)
-    def _():
-        im_ref[...] = base_ref[...]
-
     terms = []
     for o in range(batch):
         t = target[j * batch + o]
-        low_u = low_u_ref[o]
-        wh, wl = split(nt_dot(sh_ref[t], low_u) + nt_dot(sl_ref[t], low_u))
+        wh, wl = split(nt_dot(sk_ref[t], low_u_ref[o]))
         mixing = mix_ref[o]
         ph, pll = split(nn_dot(wh, mixing) + nn_dot(wl, mixing))
         v = v_refs[o][0]
         terms.append((t, nn_dot(ph, v) + nn_dot(pll, v)))
     for t, y in terms:
         add_columns(im_ref, t, y)
+
+    @pl.when(j < slots)
+    def _():
+        t = near_target[j]
+        sk = sk_ref[t]
+        ph, pll = split(nt_dot(sk, lh_ref[0]) + nt_dot(sk, ll_ref[0]))
+        v = nv_ref[0]
+        add_columns(im_ref, t, nn_dot(ph, v) + nn_dot(pll, v))
 
 
 def chol_inv_kernel(s_ref, out_ref, a_ref):
@@ -298,7 +285,7 @@
     for t in range(tiles):
         s = s_ref[t]
         a_ref[t, :, :r] = lax.dot_general(
-            s, s, (((1,), (1,)), ((), ())), precision=HIGHEST, preferred_element_type=F32
+            s, s, (((1,), (1,)), ((), ())), preferred_element_type=F32
         )
         a_ref[t, :, r:] = eye
     rows = [a_ref[:, 8 * b : 8 * b + 8, :] for b in range(r // 8)]
@@ -326,6 +313,19 @@
 
 def at_right(shape, batch, o):
     return pl.BlockSpec((1,) + shape[1:], lambda j, right, *s: (right[j * batch + o], 0, 0))
+
+
+def at_near(shape, slots):
+    return pl.BlockSpec(
+        (1,) + shape[1:],
+        lambda j, right, target, near, *s: (near[jnp.minimum(j, slots - 1)], 0, 0),
+    )
+
+
+def near_step(shape):
+    return pl.BlockSpec(
+        (1,) + shape[1:], lambda j, *s: (jnp.minimum(j, shape[0] - 1), 0, 0)
+    )
 
 
 def per_step(batch, shape):
@@ -363,64 +363,42 @@
     tiles = probe_seed.shape[0]
     share = order // ni
     batch = math.gcd(lows, 4)
+    while lows // batch < slots:
+        batch = batch // 2
+    steps = lows // batch
     seg_u, seg_v = gather_tiles(nt, right_u, right_v)
     probe = probe_table(probe_seed, r, order)
     sk = jax.ShapeDtypeStruct((tiles, r, order), F32)
     left = jax.ShapeDtypeStruct((slots, r, order), BF16)
-    lh, ll, near_sk = run(
-        near_sketch_kernel,
-        (near_right, near_target, near_count),
-        slots,
-        (near_tiles, seg_u, seg_v, probe),
-        [
-            per_step(1, near_tiles.shape),
-            at_right(seg_u.shape, 1, 0),
-            at_right(seg_v.shape, 1, 0),
-            whole(probe.shape),
-        ],
-        (left, left, sk),
-        (per_step(1, left.shape), per_step(1, left.shape), whole(sk.shape)),
-    )
-    mix_shape = jax.ShapeDtypeStruct((lows, r, r), BF16)
-    mixing, sketch = run(
-        functools.partial(low_sketch_kernel, batch),
-        (low_right, low_target),
-        lows // batch,
-        (seg_u,) * batch + (seg_v,) * batch + (low_u, low_v, probe, near_sk),
+    mix = jax.ShapeDtypeStruct((lows, r, r), BF16)
+    near_specs = [at_near(seg_v.shape, slots)]
+    mixing, lh, ll, sketch = run(
+        functools.partial(sketch_kernel, batch, slots),
+        (low_right, low_target, near_right, near_target, near_count),
+        steps,
+        (seg_u,) * batch + (seg_v,) * batch + (low_u, low_v, near_tiles, seg_u, seg_v, probe),
         [at_right(seg_u.shape, batch, o) for o in range(batch)] * 2
         + [per_step(batch, low_u.shape), per_step(batch, low_v.shape)]
-        + [whole(probe.shape), whole(sk.shape)],
-        (mix_shape, sk),
-        (per_step(batch, mix_shape.shape), whole(sk.shape)),
+        + [near_step(near_tiles.shape)]
+        + near_specs * 2
+        + [whole(probe.shape)],
+        (mix, left, left, sk),
+        (per_step(batch, mix.shape), near_step(left.shape), near_step(left.shape), whole(sk.shape)),
     )
     rows = tiles * r // ni
     total = reduce_inner(ni, sketch.reshape(ni // 2, 2, rows, order), True)
     total = total.reshape(tiles, r, order)
-    sh, sl = split(total)
     im = jax.ShapeDtypeStruct((ni, tiles, r, share), F32)
-    near_im = run(
-        near_image_kernel,
-        (near_right, near_target),
-        slots,
-        (lh, ll, seg_v, sh, sl),
-        [
-            per_step(1, lh.shape),
-            per_step(1, ll.shape),
-            at_right(seg_v.shape, 1, 0),
-            whole(sh.shape),
-            whole(sl.shape),
-        ],
-        im,
-        whole(im.shape),
-    )
     image = run(
-        functools.partial(low_image_kernel, batch),
-        (low_right, low_target),
-        lows // batch,
-        (seg_v,) * batch + (low_u, mixing, sh, sl, near_im),
+        functools.partial(image_kernel, batch, slots),
+        (low_right, low_target, near_right, near_target),
+        steps,
+        (seg_v,) * batch + (low_u, mixing, lh, ll, seg_v, total),
         [at_right(seg_v.shape, batch, o) for o in range(batch)]
         + [per_step(batch, low_u.shape), per_step(batch, mixing.shape)]
-        + [whole(sh.shape), whole(sl.shape), whole(im.shape)],
+        + [near_step(lh.shape), near_step(ll.shape)]
+        + near_specs
+        + [whole(total.shape)],
         im,
         whole(im.shape),
     )
@@ -432,7 +410,7 @@
     )(total)
     summed = reduce_inner(ni, image.reshape(ni // 2, 2, tiles * r, share), False)
     summed = summed.reshape(tiles, r, share)
-    mine = lax.dynamic_slice_in_dim(total, lax.axis_index("inner") * share, share, 2)
+    mine = lax.dynamic_slice_in_dim(total, lax.axis_index("inner") * share, share, 2).astype(F32)
     basis = jnp.einsum("tde,tei->tdi", inverse, mine, precision=HIGHEST)
     image_out = jnp.einsum("tde,tei->tdi", inverse, summed, precision=HIGHEST)
     return (basis * math.sqrt(order), image_out)

time: 238 us -> 187 us (0.79)
  Pallas kernels: 225 us -> 177 us
  other arithmetic: 7.3 us -> 3.2 us
    pallas_call x2, Pallas kernels: 87.5 us -> 53.1 us  [reduce_inner(): pl.pallas_call(functools.partial(reduce_kernel, n, gather), out_shape=jax...]
    pallas_call x4 -> x2, Pallas kernels: 55.8 us -> 44.9 us  [run(): pl.pallas_call(kernel, grid_spec=pltpu.PrefetchScalarGridSpec(num_scalar_...]
    convert_element_type x2 -> x0, other arithmetic: 4.04 us -> none  [the longest x1 2.88 us: split(): hi = x.astype(BF16)]
where the time goes in v1:
time: 187 us; the launch traced here: 186 us
  Pallas kernels  177 us (95%)
  matrix products  4.05 us (2%)
  other arithmetic  3.2 us (2%)
    pallas_call x1, Pallas kernels, gather_tiles(): pl.pallas_call(functools.partial(gather_kernel, nt), out_shape=(shape, sh...  70.4 us
    pallas_call x2, Pallas kernels, reduce_inner(): pl.pallas_call(functools.partial(reduce_kernel, n, gather), out_shape=jax...  53.1 us
    pallas_call x2, Pallas kernels, run(): pl.pallas_call(kernel, grid_spec=pltpu.PrefetchScalarGridSpec(num_scalar_...  44.9 us
    pallas_call x1, Pallas kernels, per_device(): pl.pallas_call(chol_inv_kernel, out_shape=jax.ShapeDtypeStruct((tiles, r,...  8.98 us

profile of v1, /device:TPU:9, one launch (start us, length us, event | category | flops | bytes accessed | tf_op | source)
XLA Modules:
  0.0 186.0 jit_solution(9420912575027682322)
XLA Ops:
  0.7 0.7 broadcast_multiply_fusion
  1.3 2.5 %fusion.3.refs_13_ = bf16[8,64,1024]{2,1,0:T(8,128)(2,1)} fusion(s32[64]{0:T(128)S(1)} %get-tuple-element.16, s32[1024]{0:T(1024)S(1)} %get-tuple-element.14, s32[64]{0:T(128)S(1)} %get-tuple-element.17, s32[1024]{0:T(1024)S(1)} %get-tuple-element.15, s32[8]{0:T(128)S(1)} %broadcast_multiply_fusion), kind=kLoop, calls=%fused_computation.4 | loop fusion | flops 8912896 | bytes 1057312 | tf_op jit(solution)/shard_map/convert_element_type | solution.py:43
  3.8 70.4 %shard_map.122 = (bf16[32,64,1024]{2,1,0:T(8,128)(2,1)}, bf16[32,64,1024]{2,1,0:T(8,128)(2,1)}) custom-call(bf16[8,64,1024]{2,1,0:T(8,128)(2,1)} %u_ref.1, bf16[8,64,1024]{2,1,0:T(8,128)(2,1)} %v_ref.1), custom_call_target="tpu_custom_call" | custom-call | tf_op jit(solution)/shard_map/pallas_call | solution.py:109
  74.9 26.5 %shard_map.123 = (bf16[32,64,64]{2,1,0:T(8,128)(2,1)}, bf16[4,64,1024]{2,1,0:T(8,128)(2,1)}, bf16[4,64,1024]{2,1,0:T(8,128)(2,1)}, f32[8,64,1024]{2,1,0:T(8,128)}) custom-call(s32[32]{0:T(128)} %right.3, s32[32]{0:T(128)} %target.3, s32[4]{0:T(128)} %near_right.3, s32[4]{0:T(128)} %near_target.3, s32[1]{0:T(128)S(6)} %copy.13.count, ...), custom_call_target="tpu_custom_call" | custom-call | tf_op jit(solution)/shard_map/pallas_call | solution.py:336
  101.4 32.8 %shard_map.124 = bf16[4,2,64,1024]{3,2,1,0:T(8,128)(2,1)} custom-call(f32[4,2,64,1024]{3,2,1,0:T(8,128)} %bitcast.11), custom_call_target="tpu_custom_call" | custom-call | tf_op jit(solution)/shard_map/pallas_call | solution.py:193
  134.2 18.4 %shard_map.126 = f32[8,8,64,128]{3,2,1,0:T(8,128)} custom-call(s32[32]{0:T(128)} %right.3, s32[32]{0:T(128)} %target.3, s32[4]{0:T(128)} %near_right.3, s32[4]{0:T(128)} %near_target.3, bf16[32,64,1024]{2,1,0:T(8,128)(2,1)} %get-tuple-element.9.refs_4_.refs_5_.refs_6_.refs_7_.refs_12_.refs_0_.refs_1_.refs_2_.refs_3_.refs_8_, ...), custom_call_target="tpu_custom_call" | custom-call | tf_op jit(solution)/shard_map/pallas_call | solution.py:336
  152.6 20.3 %shard_map.127 = f32[512,128]{1,0:T(8,128)} custom-call(f32[4,2,512,128]{3,2,1,0:T(8,128)} %bitcast.10), custom_call_target="tpu_custom_call" | custom-call | tf_op jit(solution)/shard_map/pallas_call | solution.py:193
  172.9 9.0 %shard_map.125 = f32[8,64,64]{2,1,0:T(8,128)} custom-call(bf16[8,64,1024]{2,1,0:T(8,128)(2,1)} %bitcast.8), custom_call_target="tpu_custom_call" | custom-call | tf_op jit(solution)/shard_map/pallas_call | solution.py:405
  181.9 2.1 %fusion.9 = f32[8,64,128]{2,1,0:T(8,128)} fusion(f32[8,64,64]{2,1,0:T(8,128)} %shard_map.125, f32[8,64,128]{2,1,0:T(8,128)} %bitcast.12), kind=kOutput, calls=%fused_computation.17 | convolution fusion | flops 50331648 | bytes 655360 | tf_op jit(solution)/shard_map/tde,tei->tdi/dot_general | solution.py:415
  184.0 1.9 %convolution_multiply_fusion = f32[8,64,128]{2,1,0:T(8,128)} fusion(f32[8,64,64]{2,1,0:T(8,128)} %shard_map.125, bf16[8,64,1024]{2,1,0:T(8,128)(2,1)} %bitcast.9, s32[]{:T(128)S(6)} %select_n.11), kind=kOutput, calls=%fused_computation.9 | convolution fusion | flops 50397184 | bytes 655364 | tf_op jit(solution)/shard_map/tde,tei->tdi/dot_general | solution.py:414
  (2 shorter events, 0.0 us)

commit v2 on v1

--- a/solution.py
+++ b/solution.py
@@ -43,14 +43,20 @@
     return ((code.astype(F32) - 32760.0) / 32768.0).astype(BF16)
 
 
-def gather_kernel(nt, u_ref, v_ref, su_ref, sv_ref, send, recv, local):
+def gather_kernel(nt, batch, low_right, near_right, count, u_ref, v_ref, low_v_ref, near_ref, *refs):
+    sv_ref, mix_ref, lh_ref, ll_ref, su, sv, low_v, near, send, recv, local, out_sem = refs
     me = lax.axis_index("tgt")
     k = u_ref.shape[0]
+    h = k // 2
     mine = pl.ds(me * k, k)
-    lu = pltpu.make_async_copy(u_ref, su_ref.at[mine], local.at[0])
-    lv = pltpu.make_async_copy(v_ref, sv_ref.at[mine], local.at[1])
-    lu.start()
-    lv.start()
+    loads = [
+        pltpu.make_async_copy(u_ref, su.at[mine], local.at[0]),
+        pltpu.make_async_copy(v_ref, sv.at[mine], local.at[1]),
+        pltpu.make_async_copy(low_v_ref, low_v, local.at[2]),
+        pltpu.make_async_copy(near_ref, near, local.at[3]),
+    ]
+    for c in loads:
+        c.start()
     barrier = pltpu.get_barrier_semaphore()
 
     def push(src, dst, sem, to):
@@ -65,66 +71,158 @@
         copy.start()
         return copy
 
-    copies = []
+    def mix():
+        loads[2].wait()
+
+        def body(i, carry):
+            for o in range(batch):
+                j = i * batch + o
+                mix_ref[j] = nt_dot(low_v[j], su[low_right[j]]).astype(BF16)
+            return carry
+
+        lax.fori_loop(0, low_v.shape[0] // batch, body, 0)
+
+    def lefts():
+        loads[3].wait()
+
+        def body(j, carry):
+            live = (j < count[0]).astype(F32)
+            hi, lo = split(nt_dot(su[near_right[j]], near[j]) * live)
+            lh_ref[j] = hi
+            ll_ref[j] = lo
+            return carry
+
+        lax.fori_loop(0, near.shape[0], body, 0)
+
     if nt == 4:
         a = me + 1 - 2 * (me % 2)
         b = (me + 2) % 4
         for peer in (a, b):
             pl.semaphore_signal(barrier, inc=1, device_id={"tgt": peer}, device_id_type=MESH)
         pl.semaphore_wait(barrier, 2)
-        ua = push(u_ref, su_ref.at[mine], 0, a)
-        vb = push(v_ref, sv_ref.at[mine], 1, b)
-        va = push(v_ref, sv_ref.at[mine], 2, a)
-        ub = push(u_ref, su_ref.at[mine], 3, b)
-        from_a = pl.ds(a * k, k)
-        from_b = pl.ds(b * k, k)
-        ua.wait_recv()
-        fu = push(su_ref.at[from_a], su_ref.at[from_a], 4, b)
-        vb.wait_recv()
-        fv = push(sv_ref.at[from_b], sv_ref.at[from_b], 5, a)
-        for c in (va, ub, fu, fv):
+
+        def own(src, dst, sem):
+            low, high = pl.ds(0, h), pl.ds(h, k - h)
+            at_low, at_high = pl.ds(me * k, h), pl.ds(me * k + h, k - h)
+            return [
+                push(src.at[low], dst.at[at_low], sem, a),
+                push(src.at[high], dst.at[at_high], sem + 1, b),
+                push(src.at[high], dst.at[at_high], sem + 2, a),
+                push(src.at[low], dst.at[at_low], sem + 3, b),
+            ]
+
+        def onward(dst, copies, sem):
+            from_a, from_b = pl.ds(a * k, h), pl.ds(b * k + h, k - h)
+            copies[0].wait_recv()
+            fa = push(dst.at[from_a], dst.at[from_a], sem, b)
+            copies[1].wait_recv()
+            return [fa, push(dst.at[from_b], dst.at[from_b], sem + 1, a)]
+
+        us = own(u_ref, su, 0)
+        uf = onward(su, us, 4)
+        vs = own(v_ref, sv, 6)
+        for c in us[2:] + uf:
             c.wait_recv()
-        copies = [ua, vb, va, ub, fu, fv]
+        loads[0].wait()
+        mix()
+        vf = onward(sv, vs, 10)
+        lefts()
+        for c in vs[2:] + vf:
+            c.wait_recv()
+        copies = us + uf + vs + vf
     else:
         for d in range(1, nt):
             pl.semaphore_signal(
                 barrier, inc=1, device_id={"tgt": (me + d) % nt}, device_id_type=MESH
             )
         pl.semaphore_wait(barrier, nt - 1)
+        copies = []
         for d in range(1, nt):
             to = (me + d) % nt
-            copies.append(push(u_ref, su_ref.at[mine], 2 * d - 2, to))
-            copies.append(push(v_ref, sv_ref.at[mine], 2 * d - 1, to))
+            copies.append(push(u_ref, su.at[mine], 2 * d - 2, to))
+            copies.append(push(v_ref, sv.at[mine], 2 * d - 1, to))
         for c in copies:
             c.wait_recv()
+        loads[0].wait()
+        mix()
+        lefts()
+    loads[1].wait()
+    out = pltpu.make_async_copy(sv, sv_ref, out_sem)
+    out.start()
     for c in copies:
         c.wait_send()
-    lu.wait()
-    lv.wait()
-
-
-def gather_tiles(nt, u, v):
-    sems = 6 if nt == 4 else max(2 * nt - 2, 1)
-    shape = jax.ShapeDtypeStruct((nt * u.shape[0],) + u.shape[1:], u.dtype)
+    out.wait()
+
+
+def gather_tiles(nt, batch, low_right, near_right, count, u, v, low_v, near):
+    sems = 12 if nt == 4 else max(2 * nt - 2, 1)
+    seg = (nt * u.shape[0],) + u.shape[1:]
+    r = u.shape[1]
+    left = jax.ShapeDtypeStruct((near.shape[0], r, near.shape[1]), BF16)
     return pl.pallas_call(
-        functools.partial(gather_kernel, nt),
-        out_shape=(shape, shape),
-        in_specs=[pl.BlockSpec(memory_space=pl.ANY)] * 2,
-        out_specs=[pl.BlockSpec(memory_space=pl.ANY)] * 2,
+        functools.partial(gather_kernel, nt, batch),
+        out_shape=(
+            jax.ShapeDtypeStruct(seg, v.dtype),
+            jax.ShapeDtypeStruct((low_v.shape[0], low_v.shape[1], r), BF16),
+            left,
+            left,
+        ),
+        in_specs=[pl.BlockSpec(memory_space=pltpu.SMEM)] * 3
+        + [pl.BlockSpec(memory_space=pl.ANY)] * 4,
+        out_specs=[pl.BlockSpec(memory_space=pl.ANY)]
+        + [pl.BlockSpec(memory_space=pltpu.VMEM)] * 3,
         scratch_shapes=[
+            pltpu.VMEM(seg, u.dtype),
+            pltpu.VMEM(seg, v.dtype),
+            pltpu.VMEM(low_v.shape, low_v.dtype),
+            pltpu.VMEM(near.shape, near.dtype),
             pltpu.SemaphoreType.DMA((sems,)),
             pltpu.SemaphoreType.DMA((sems,)),
-            pltpu.SemaphoreType.DMA((2,)),
+            pltpu.SemaphoreType.DMA((4,)),
+            pltpu.SemaphoreType.DMA,
         ],
-        compiler_params=pltpu.CompilerParams(collective_id=0, has_side_effects=True),
-    )(u, v)
+        compiler_params=pltpu.CompilerParams(
+            collective_id=0, has_side_effects=True, vmem_limit_bytes=VMEM_LIMIT
+        ),
+    )(low_right, near_right, count, u, v, low_v, near)
+
+
+def chol_inverse(s_ref, out_ref, a_ref):
+    tiles, r, _ = s_ref.shape
+    row = lax.broadcasted_iota(jnp.int32, (r, r), 0)
+    col = lax.broadcasted_iota(jnp.int32, (r, r), 1)
+    eye = (row == col).astype(F32)
+    for t in range(tiles):
+        s = s_ref[t]
+        a_ref[t, :, :r] = nt_dot(s, s)
+        a_ref[t, :, r:] = eye
+    for base in range(0, r, 8):
+        shape = (tiles, r - base, 2 * r)
+        sub = lax.broadcasted_iota(jnp.int32, shape, 1) + base
+        lane = lax.broadcasted_iota(jnp.int32, shape, 2)
+
+        def body(k, carry):
+            whole_a = a_ref[:, base:, :]
+            pivot = a_ref[:, pl.ds(k, 1), :]
+            column = jnp.sum(jnp.where(lane == k, whole_a, 0.0), axis=2, keepdims=True)
+            diag = jnp.sum(jnp.where(lane[:, :1] == k, pivot, 0.0), axis=2, keepdims=True)
+            step = column * (pivot / diag)
+            a_ref[:, base:, :] = whole_a - jnp.where(sub > k, step, 0.0)
+            return carry
+
+        lax.fori_loop(base, base + 8, body, 0)
+    a = a_ref[...]
+    sub = lax.broadcasted_iota(jnp.int32, a.shape, 1)
+    lane = lax.broadcasted_iota(jnp.int32, a.shape, 2)
+    diag = jnp.sum(jnp.where(lane == sub, a, 0.0), axis=2, keepdims=True)
+    out_ref[...] = (a * lax.rsqrt(diag))[:, :, r:]
 
 
 def reduce_kernel(n, gather, x_ref, *refs):
     if gather:
         out_ref, half, cut, part, total, send, recv = refs
     else:
-        out_ref, half, cut, part, send, recv = refs
+        s_ref, out_ref, inv_ref, half, cut, part, a_ref, send, recv = refs
     me = lax.axis_index("inner")
     m = n // 2
     z = me // 2
@@ -161,6 +259,8 @@
         if d < m - 1:
             cut[d] = (half[q] + x_ref[q, core]).astype(BF16)
             sends.append(push(cut.at[d], part.at[m - 2 - d], m + d, q * 2 + core))
+    if not gather:
+        chol_inverse(s_ref, inv_ref, a_ref)
     acc = half[z] + x_ref[z, core]
     for d in range(m - 1):
         sends[d].wait_recv()
@@ -186,32 +286,36 @@
         c.wait_send()
 
 
-def reduce_inner(n, x, gather):
+def reduce_inner(n, x, gather, sketch=None):
     m = n // 2
     block = x.shape[2:]
     sems = 4 * m - 2 if gather else 2 * m - 1
+    args = [x] if gather else [x, sketch]
+    scratch = [pltpu.VMEM((m,) + block, F32)] + [pltpu.VMEM((max(m - 1, 1),) + block, BF16)] * 2
+    vmem = pl.BlockSpec(memory_space=pltpu.VMEM)
+    if gather:
+        outs, specs = jax.ShapeDtypeStruct(x.shape, BF16), vmem
+        scratch.append(pltpu.VMEM(block, BF16))
+    else:
+        tiles, r, _ = sketch.shape
+        outs = (jax.ShapeDtypeStruct(block, F32), jax.ShapeDtypeStruct((tiles, r, r), F32))
+        specs = (vmem, vmem)
+        scratch.append(pltpu.VMEM((tiles, r, 2 * r), F32))
     return pl.pallas_call(
         functools.partial(reduce_kernel, n, gather),
-        out_shape=jax.ShapeDtypeStruct(x.shape, BF16) if gather else jax.ShapeDtypeStruct(block, F32),
-        in_specs=[pl.BlockSpec(memory_space=pltpu.VMEM)],
-        out_specs=pl.BlockSpec(memory_space=pltpu.VMEM),
-        scratch_shapes=[
-            pltpu.VMEM((m,) + block, F32),
-            pltpu.VMEM((max(m - 1, 1),) + block, BF16),
-            pltpu.VMEM((max(m - 1, 1),) + block, BF16),
-        ]
-        + ([pltpu.VMEM(block, BF16)] if gather else [])
-        + [pltpu.SemaphoreType.DMA((sems,)), pltpu.SemaphoreType.DMA((sems,))],
+        out_shape=outs,
+        in_specs=[vmem] * len(args),
+        out_specs=specs,
+        scratch_shapes=scratch + [pltpu.SemaphoreType.DMA((sems,))] * 2,
         compiler_params=pltpu.CompilerParams(
             collective_id=1 if gather else 2, has_side_effects=True, vmem_limit_bytes=VMEM_LIMIT
         ),
-    )(x)
-
-
-def sketch_kernel(batch, slots, right, target, near_right, near_target, count, *refs):
-    u_refs, v_refs = refs[:batch], refs[batch : 2 * batch]
-    low_u_ref, low_v_ref, near_ref, nu_ref, nv_ref, probe_ref = refs[2 * batch : 2 * batch + 6]
-    mix_ref, lh_ref, ll_ref, sk_ref = refs[2 * batch + 6 :]
+    )(*args)
+
+
+def sketch_kernel(batch, slots, right, target, near_right, near_target, *refs):
+    v_refs = refs[:batch]
+    low_u_ref, mix_ref, lh_ref, ll_ref, nv_ref, probe_ref, sk_ref = refs[batch:]
     j = pl.program_id(0)
 
     @pl.when(j == 0)
@@ -221,8 +325,7 @@
     terms = []
     for o in range(batch):
         t = target[j * batch + o]
-        mixing = nt_dot(low_v_ref[o], u_refs[o][0]).astype(BF16)
-        mix_ref[o] = mixing
+        mixing = mix_ref[o]
         zh, zl = split(nt_dot(probe_ref[t], v_refs[o][0]))
         qh, ql = split(nt_dot(zh, mixing) + nt_dot(zl, mixing))
         low_u = low_u_ref[o]
@@ -233,13 +336,9 @@
     @pl.when(j < slots)
     def _():
         t = near_target[j]
-        live = (j < count[0]).astype(F32)
-        left = nt_dot(nu_ref[0], near_ref[0]) * live
-        lh, ll = split(left)
-        lh_ref[0] = lh
-        ll_ref[0] = ll
+        lh = lh_ref[0]
         zh, zl = split(nt_dot(probe_ref[t], nv_ref[0]))
-        sk_ref[t] += nn_dot(zh, lh) + nn_dot(zl, lh) + nn_dot(zh, ll)
+        sk_ref[t] += nn_dot(zh, lh) + nn_dot(zl, lh) + nn_dot(zh, ll_ref[0])
 
 
 def add_columns(im_ref, t, y):
@@ -275,35 +374,6 @@
         ph, pll = split(nt_dot(sk, lh_ref[0]) + nt_dot(sk, ll_ref[0]))
         v = nv_ref[0]
         add_columns(im_ref, t, nn_dot(ph, v) + nn_dot(pll, v))
-
-
-def chol_inv_kernel(s_ref, out_ref, a_ref):
-    tiles, r, _ = s_ref.shape
-    row = lax.broadcasted_iota(jnp.int32, (r, r), 0)
-    col = lax.broadcasted_iota(jnp.int32, (r, r), 1)
-    eye = (row == col).astype(F32)
-    for t in range(tiles):
-        s = s_ref[t]
-        a_ref[t, :, :r] = lax.dot_general(
-            s, s, (((1,), (1,)), ((), ())), preferred_element_type=F32
-        )
-        a_ref[t, :, r:] = eye
-    rows = [a_ref[:, 8 * b : 8 * b + 8, :] for b in range(r // 8)]
-    sub = lax.broadcasted_iota(jnp.int32, (tiles, 8, 2 * r), 1)
-    for k in range(r):
-        b0, e = k // 8, k % 8
-        pivot = rows[b0][:, e : e + 1, :]
-        inv = 1.0 / pivot[:, :, k : k + 1]
-        scaled = pivot * inv
-        for b in range(b0, r // 8):
-            step = rows[b][:, :, k : k + 1] * scaled
-            if b == b0:
-                step = jnp.where(sub > e, step, 0.0)
-            rows[b] = rows[b] - step
-    lane = lax.broadcasted_iota(jnp.int32, (tiles, 8, 2 * r), 2)
-    for b in range(r // 8):
-        diag = jnp.sum(jnp.where(lane == sub + 8 * b, rows[b], 0.0), axis=2, keepdims=True)
-        out_ref[:, 8 * b : 8 * b + 8, :] = (rows[b] * lax.rsqrt(diag))[:, :, r:]
 
 
 def whole(shape):
@@ -366,24 +436,28 @@
     while lows // batch < slots:
         batch = batch // 2
     steps = lows // batch
-    seg_u, seg_v = gather_tiles(nt, right_u, right_v)
+    seg_v, mixing, lh, ll = gather_tiles(
+        nt, batch, low_right, near_right, near_count, right_u, right_v, low_v, near_tiles
+    )
     probe = probe_table(probe_seed, r, order)
     sk = jax.ShapeDtypeStruct((tiles, r, order), F32)
-    left = jax.ShapeDtypeStruct((slots, r, order), BF16)
-    mix = jax.ShapeDtypeStruct((lows, r, r), BF16)
     near_specs = [at_near(seg_v.shape, slots)]
-    mixing, lh, ll, sketch = run(
+    pair_specs = (
+        [at_right(seg_v.shape, batch, o) for o in range(batch)]
+        + [per_step(batch, low_u.shape), per_step(batch, mixing.shape)]
+        + [near_step(lh.shape), near_step(ll.shape)]
+        + near_specs
+    )
+    scalars = (low_right, low_target, near_right, near_target)
+    pair_args = (seg_v,) * batch + (low_u, mixing, lh, ll, seg_v)
+    sketch = run(
         functools.partial(sketch_kernel, batch, slots),
-        (low_right, low_target, near_right, near_target, near_count),
+        scalars,
         steps,
-        (seg_u,) * batch + (seg_v,) * batch + (low_u, low_v, near_tiles, seg_u, seg_v, probe),
-        [at_right(seg_u.shape, batch, o) for o in range(batch)] * 2
-        + [per_step(batch, low_u.shape), per_step(batch, low_v.shape)]
-        + [near_step(near_tiles.shape)]
-        + near_specs * 2
-        + [whole(probe.shape)],
-        (mix, left, left, sk),
-        (per_step(batch, mix.shape), near_step(left.shape), near_step(left.shape), whole(sk.shape)),
+        pair_args + (probe,),
+        pair_specs + [whole(probe.shape)],
+        sk,
+        whole(sk.shape),
     )
     rows = tiles * r // ni
     total = reduce_inner(ni, sketch.reshape(ni // 2, 2, rows, order), True)
@@ -391,24 +465,16 @@
     im = jax.ShapeDtypeStruct((ni, tiles, r, share), F32)
     image = run(
         functools.partial(image_kernel, batch, slots),
-        (low_right, low_target, near_right, near_target),
+        scalars,
         steps,
-        (seg_v,) * batch + (low_u, mixing, lh, ll, seg_v, total),
-        [at_right(seg_v.shape, batch, o) for o in range(batch)]
-        + [per_step(batch, low_u.shape), per_step(batch, mixing.shape)]
-        + [near_step(lh.shape), near_step(ll.shape)]
-        + near_specs
-        + [whole(total.shape)],
+        pair_args + (total,),
+        pair_specs + [whole(total.shape)],
         im,
         whole(im.shape),
     )
-    inverse = pl.pallas_call(
-        chol_inv_kernel,
-        out_shape=jax.ShapeDtypeStruct((tiles, r, r), F32),
-        scratch_shapes=[pltpu.VMEM((tiles, r, 2 * r), F32)],
-        compiler_params=pltpu.CompilerParams(vmem_limit_bytes=VMEM_LIMIT),
-    )(total)
-    summed = reduce_inner(ni, image.reshape(ni // 2, 2, tiles * r, share), False)
+    summed, inverse = reduce_inner(
+        ni, image.reshape(ni // 2, 2, tiles * r, share), False, total
+    )
     summed = summed.reshape(tiles, r, share)
     mine = lax.dynamic_slice_in_dim(total, lax.axis_index("inner") * share, share, 2).astype(F32)
     basis = jnp.einsum("tde,tei->tdi", inverse, mine, precision=HIGHEST)

time: 187 us -> 175 us (0.936)
  Pallas kernels: 177 us -> 166 us
    pallas_call x2, Pallas kernels: 44.9 us -> 38.5 us  [run(): pl.pallas_call(kernel, grid_spec=pltpu.PrefetchScalarGridSpec(num_scalar_...]
    pallas_call x4 -> x3, Pallas kernels: 133 us -> 128 us  [the longest x1 74.3 us: gather_tiles(): pl.pallas_call(functools.partial(gather_kernel, nt, batch), out_shape=(ja...]
where the time goes in v2:
time: 175 us; the launch traced here: 174 us
  Pallas kernels  166 us (95%)
  matrix products  4.05 us (2%)
  other arithmetic  2.57 us (1%)
    pallas_call x1, Pallas kernels, gather_tiles(): pl.pallas_call(functools.partial(gather_kernel, nt, batch), out_shape=(ja...  74.3 us
    pallas_call x2, Pallas kernels, reduce_inner(): pl.pallas_call(functools.partial(reduce_kernel, n, gather), out_shape=out...  53.4 us
    pallas_call x2, Pallas kernels, run(): pl.pallas_call(kernel, grid_spec=pltpu.PrefetchScalarGridSpec(num_scalar_...  38.5 us

profile of v2, /device:TPU:9, one launch (start us, length us, event | category | flops | bytes accessed | tf_op | source)
XLA Modules:
  0.0 174.2 jit_solution(12643734787533348188)
XLA Ops:
  1.3 0.0 copy-start
  1.3 74.3 %shard_map.122 = (bf16[32,64,1024]{2,1,0:T(8,128)(2,1)}, bf16[32,64,64]{2,1,0:T(8,128)(2,1)}, bf16[4,64,1024]{2,1,0:T(8,128)(2,1)}, bf16[4,64,1024]{2,1,0:T(8,128)(2,1)}) custom-call(s32[32]{0:T(128)} %right.3, s32[4]{0:T(128)} %near_right.5, s32[1]{0:T(128)S(6)} %copy.13.count, bf16[8,64,1024]{2,1,0:T(8,128)(2,1)} %u_ref.1, bf16[8,64,1024]{2,1,0:T(8,128)(2,1)} %v_ref.1, ...), custom_call_target="tpu_custom_call" | custom-call | tf_op jit(solution)/shard_map/pallas_call | solution.py:162
  75.6 0.0 copy-done
  75.7 2.6 %fusion.3.refs_9_ = bf16[8,64,1024]{2,1,0:T(8,128)(2,1)} fusion(s32[64]{0:T(128)S(1)} %get-tuple-element.16, s32[1024]{0:T(1024)S(1)} %get-tuple-element.14, s32[64]{0:T(128)S(1)} %get-tuple-element.17, s32[1024]{0:T(1024)S(1)} %get-tuple-element.15, s32[8]{0:T(128)S(1)} %broadcast_multiply_fusion), kind=kLoop, calls=%fused_computation.4 | loop fusion | flops 8912896 | bytes 1057312 | tf_op jit(solution)/shard_map/convert_element_type | solution.py:43
  78.2 20.2 %shard_map.123 = f32[8,64,1024]{2,1,0:T(8,128)} custom-call(s32[32]{0:T(128)} %right.3, s32[32]{0:T(128)} %target.3, s32[4]{0:T(128)} %near_right.5, s32[4]{0:T(128)} %near_target.3, bf16[32,64,1024]{2,1,0:T(8,128)(2,1)} %get-tuple-element.8.refs_0_.refs_1_.refs_2_.refs_3_.refs_8_, ...), custom_call_target="tpu_custom_call" | custom-call | tf_op jit(solution)/shard_map/pallas_call | solution.py:406
  98.4 32.6 %shard_map.124 = bf16[4,2,64,1024]{3,2,1,0:T(8,128)(2,1)} custom-call(f32[4,2,64,1024]{3,2,1,0:T(8,128)} %bitcast.11), custom_call_target="tpu_custom_call" | custom-call | tf_op jit(solution)/shard_map/pallas_call | solution.py:304
  131.0 18.4 %shard_map.125 = f32[8,8,64,128]{3,2,1,0:T(8,128)} custom-call(s32[32]{0:T(128)} %right.3, s32[32]{0:T(128)} %target.3, s32[4]{0:T(128)} %near_right.5, s32[4]{0:T(128)} %near_target.3, bf16[32,64,1024]{2,1,0:T(8,128)(2,1)} %get-tuple-element.8.refs_0_.refs_1_.refs_2_.refs_3_.refs_8_, ...), custom_call_target="tpu_custom_call" | custom-call | tf_op jit(solution)/shard_map/pallas_call | solution.py:406
  149.4 20.8 %shard_map.126 = (f32[512,128]{1,0:T(8,128)}, f32[8,64,64]{2,1,0:T(8,128)}) custom-call(f32[4,2,512,128]{3,2,1,0:T(8,128)} %bitcast.10, bf16[8,64,1024]{2,1,0:T(8,128)(2,1)} %bitcast.8), custom_call_target="tpu_custom_call" | custom-call | tf_op jit(solution)/shard_map/pallas_call | solution.py:304
  170.2 2.1 %fusion.9 = f32[8,64,128]{2,1,0:T(8,128)} fusion(f32[8,64,64]{2,1,0:T(8,128)} %get-tuple-element.12, f32[8,64,128]{2,1,0:T(8,128)} %bitcast.12), kind=kOutput, calls=%fused_computation.17 | convolution fusion | flops 50331648 | bytes 655360 | tf_op jit(solution)/shard_map/tde,tei->tdi/dot_general | solution.py:481
  172.3 1.9 %convolution_multiply_fusion = f32[8,64,128]{2,1,0:T(8,128)} fusion(f32[8,64,64]{2,1,0:T(8,128)} %get-tuple-element.12, bf16[8,64,1024]{2,1,0:T(8,128)(2,1)} %bitcast.9, s32[]{:T(128)S(6)} %select_n.11), kind=kOutput, calls=%fused_computation.9 | convolution fusion | flops 50397184 | bytes 655364 | tf_op jit(solution)/shard_map/tde,tei->tdi/dot_general | solution.py:480
  (3 shorter events, 0.0 us)
Async XLA Ops:
  1.3 74.4 %copy-start = (s32[8]{0:T(128)S(1)}, s32[8]{0:T(128)}, u32[]{:S(2)}) copy-start(s32[8]{0:T(128)} %param.21) | copy-start | bytes 100

commit v3 on v2

--- a/solution.py
+++ b/solution.py
@@ -313,7 +313,15 @@
     )(*args)
 
 
-def sketch_kernel(batch, slots, right, target, near_right, near_target, *refs):
+def both(x, axis):
+    return jnp.concatenate([x, x], axis=axis)
+
+
+def parts(x):
+    return jnp.concatenate(split(x), axis=1)
+
+
+def sketch_kernel(batch, slots, steps, right, target, near_right, near_target, *refs):
     v_refs = refs[:batch]
     low_u_ref, mix_ref, lh_ref, ll_ref, nv_ref, probe_ref, sk_ref = refs[batch:]
     j = pl.program_id(0)
@@ -322,23 +330,25 @@
     def _():
         sk_ref[...] = jnp.zeros_like(sk_ref)
 
-    terms = []
-    for o in range(batch):
-        t = target[j * batch + o]
-        mixing = mix_ref[o]
-        zh, zl = split(nt_dot(probe_ref[t], v_refs[o][0]))
-        qh, ql = split(nt_dot(zh, mixing) + nt_dot(zl, mixing))
-        low_u = low_u_ref[o]
-        terms.append((t, nn_dot(qh, low_u) + nn_dot(ql, low_u)))
-    for t, y in terms:
-        sk_ref[t] += y
-
-    @pl.when(j < slots)
-    def _():
+    def near_term():
         t = near_target[j]
         lh = lh_ref[0]
         zh, zl = split(nt_dot(probe_ref[t], nv_ref[0]))
-        sk_ref[t] += nn_dot(zh, lh) + nn_dot(zl, lh) + nn_dot(zh, ll_ref[0])
+        left = jnp.concatenate([lh, lh, ll_ref[0]], axis=0)
+        sk_ref[t] += nn_dot(jnp.concatenate([zh, zl, zh], axis=1), left)
+
+    span = range(batch)
+    where = [target[j * batch + o] for o in span]
+    zeta = [nt_dot(probe_ref[where[o]], v_refs[o][0]) for o in span]
+    zeta = [parts(x) for x in zeta]
+    q = [nt_dot(zeta[o], both(mix_ref[o], 1)) for o in span]
+    q = [parts(x) for x in q]
+    for o in span:
+        sk_ref[where[o]] += nn_dot(q[o], both(low_u_ref[o], 0))
+    if slots == steps:
+        near_term()
+    else:
+        pl.when(j < slots)(near_term)
 
 
 def add_columns(im_ref, t, y):
@@ -347,7 +357,7 @@
         im_ref[p, t] += y[:, p * share : (p + 1) * share]
 
 
-def image_kernel(batch, slots, right, target, near_right, near_target, *refs):
+def image_kernel(batch, slots, steps, right, target, near_right, near_target, *refs):
     v_refs = refs[:batch]
     low_u_ref, mix_ref, lh_ref, ll_ref, nv_ref, sk_ref, im_ref = refs[batch:]
     j = pl.program_id(0)
@@ -356,24 +366,24 @@
     def _():
         im_ref[...] = jnp.zeros_like(im_ref)
 
-    terms = []
-    for o in range(batch):
-        t = target[j * batch + o]
-        wh, wl = split(nt_dot(sk_ref[t], low_u_ref[o]))
-        mixing = mix_ref[o]
-        ph, pll = split(nn_dot(wh, mixing) + nn_dot(wl, mixing))
-        v = v_refs[o][0]
-        terms.append((t, nn_dot(ph, v) + nn_dot(pll, v)))
-    for t, y in terms:
-        add_columns(im_ref, t, y)
-
-    @pl.when(j < slots)
-    def _():
+    def near_term():
         t = near_target[j]
-        sk = sk_ref[t]
-        ph, pll = split(nt_dot(sk, lh_ref[0]) + nt_dot(sk, ll_ref[0]))
-        v = nv_ref[0]
-        add_columns(im_ref, t, nn_dot(ph, v) + nn_dot(pll, v))
+        left = jnp.concatenate([lh_ref[0], ll_ref[0]], axis=1)
+        proj = nt_dot(both(sk_ref[t], 1), left)
+        add_columns(im_ref, t, nn_dot(parts(proj), both(nv_ref[0], 0)))
+
+    span = range(batch)
+    where = [target[j * batch + o] for o in span]
+    w = [nt_dot(sk_ref[where[o]], low_u_ref[o]) for o in span]
+    w = [parts(x) for x in w]
+    proj = [nn_dot(w[o], both(mix_ref[o], 0)) for o in span]
+    proj = [parts(x) for x in proj]
+    for o in span:
+        add_columns(im_ref, where[o], nn_dot(proj[o], both(v_refs[o][0], 0)))
+    if slots == steps:
+        near_term()
+    else:
+        pl.when(j < slots)(near_term)
 
 
 def whole(shape):
@@ -432,7 +442,7 @@
     lows, r = low_u.shape[0], low_u.shape[1]
     tiles = probe_seed.shape[0]
     share = order // ni
-    batch = math.gcd(lows, 4)
+    batch = math.gcd(lows, 8)
     while lows // batch < slots:
         batch = batch // 2
     steps = lows // batch
@@ -451,7 +461,7 @@
     scalars = (low_right, low_target, near_right, near_target)
     pair_args = (seg_v,) * batch + (low_u, mixing, lh, ll, seg_v)
     sketch = run(
-        functools.partial(sketch_kernel, batch, slots),
+        functools.partial(sketch_kernel, batch, slots, steps),
         scalars,
         steps,
         pair_args + (probe,),
@@ -464,7 +474,7 @@
     total = total.reshape(tiles, r, order)
     im = jax.ShapeDtypeStruct((ni, tiles, r, share), F32)
     image = run(
-        functools.partial(image_kernel, batch, slots),
+        functools.partial(image_kernel, batch, slots, steps),
         scalars,
         steps,
         pair_args + (total,),

time: 175 us -> 157 us (0.90)
  Pallas kernels: 166 us -> 148 us
    pallas_call x2, Pallas kernels: 38.5 us -> 21.7 us  [run(): pl.pallas_call(kernel, grid_spec=pltpu.PrefetchScalarGridSpec(num_scalar_...]
where the time goes in v3:
time: 157 us; the launch traced here: 156 us
  Pallas kernels  148 us (94%)
  matrix products  4.05 us (3%)
  other arithmetic  2.57 us (2%)
    pallas_call x1, Pallas kernels, gather_tiles(): pl.pallas_call(functools.partial(gather_kernel, nt, batch), out_shape=(ja...  74.3 us
    pallas_call x2, Pallas kernels, reduce_inner(): pl.pallas_call(functools.partial(reduce_kernel, n, gather), out_shape=out...  52.2 us
    pallas_call x2, Pallas kernels, run(): pl.pallas_call(kernel, grid_spec=pltpu.PrefetchScalarGridSpec(num_scalar_...  21.7 us

profile of v3, /device:TPU:9, one launch (start us, length us, event | category | flops | bytes accessed | tf_op | source)
XLA Modules:
  0.0 156.1 jit_solution(10859787535145677226)
XLA Ops:
  1.3 0.0 copy-start
  1.3 74.3 %shard_map.122 = (bf16[32,64,1024]{2,1,0:T(8,128)(2,1)}, bf16[32,64,64]{2,1,0:T(8,128)(2,1)}, bf16[4,64,1024]{2,1,0:T(8,128)(2,1)}, bf16[4,64,1024]{2,1,0:T(8,128)(2,1)}) custom-call(s32[32]{0:T(128)} %right.3, s32[4]{0:T(128)} %near_right.5, s32[1]{0:T(128)S(6)} %copy.13.count, bf16[8,64,1024]{2,1,0:T(8,128)(2,1)} %u_ref.1, bf16[8,64,1024]{2,1,0:T(8,128)(2,1)} %v_ref.1, ...), custom_call_target="tpu_custom_call" | custom-call | tf_op jit(solution)/shard_map/pallas_call | solution.py:162
  75.6 0.0 copy-done
  75.7 2.6 %fusion.3.refs_13_ = bf16[8,64,1024]{2,1,0:T(8,128)(2,1)} fusion(s32[64]{0:T(128)S(1)} %get-tuple-element.16, s32[1024]{0:T(1024)S(1)} %get-tuple-element.14, s32[64]{0:T(128)S(1)} %get-tuple-element.17, s32[1024]{0:T(1024)S(1)} %get-tuple-element.15, s32[8]{0:T(128)S(1)} %broadcast_multiply_fusion), kind=kLoop, calls=%fused_computation.4 | loop fusion | flops 8912896 | bytes 1057312 | tf_op jit(solution)/shard_map/convert_element_type | solution.py:43
  78.2 10.8 %shard_map.123 = f32[8,64,1024]{2,1,0:T(8,128)} custom-call(s32[32]{0:T(128)} %right.3, s32[32]{0:T(128)} %target.3, s32[4]{0:T(128)} %near_right.5, s32[4]{0:T(128)} %near_target.3, bf16[32,64,1024]{2,1,0:T(8,128)(2,1)} %get-tuple-element.8.refs_0_.refs_1_.refs_2_.refs_3_.refs_4_.refs_5_.refs_6_.refs_7_.refs_12_, ...), custom_call_target="tpu_custom_call" | custom-call | tf_op jit(solution)/shard_map/pallas_call | solution.py:416
  89.0 32.4 %shard_map.124 = bf16[4,2,64,1024]{3,2,1,0:T(8,128)(2,1)} custom-call(f32[4,2,64,1024]{3,2,1,0:T(8,128)} %bitcast.11), custom_call_target="tpu_custom_call" | custom-call | tf_op jit(solution)/shard_map/pallas_call | solution.py:304
  121.4 10.9 %shard_map.125 = f32[8,8,64,128]{3,2,1,0:T(8,128)} custom-call(s32[32]{0:T(128)} %right.3, s32[32]{0:T(128)} %target.3, s32[4]{0:T(128)} %near_right.5, s32[4]{0:T(128)} %near_target.3, bf16[32,64,1024]{2,1,0:T(8,128)(2,1)} %get-tuple-element.8.refs_0_.refs_1_.refs_2_.refs_3_.refs_4_.refs_5_.refs_6_.refs_7_.refs_12_, ...), custom_call_target="tpu_custom_call" | custom-call | tf_op jit(solution)/shard_map/pallas_call | solution.py:416
  132.3 19.8 %shard_map.126 = (f32[512,128]{1,0:T(8,128)}, f32[8,64,64]{2,1,0:T(8,128)}) custom-call(f32[4,2,512,128]{3,2,1,0:T(8,128)} %bitcast.10, bf16[8,64,1024]{2,1,0:T(8,128)(2,1)} %bitcast.8), custom_call_target="tpu_custom_call" | custom-call | tf_op jit(solution)/shard_map/pallas_call | solution.py:304
  152.1 2.1 %fusion.9 = f32[8,64,128]{2,1,0:T(8,128)} fusion(f32[8,64,64]{2,1,0:T(8,128)} %get-tuple-element.12, f32[8,64,128]{2,1,0:T(8,128)} %bitcast.12), kind=kOutput, calls=%fused_computation.17 | convolution fusion | flops 50331648 | bytes 655360 | tf_op jit(solution)/shard_map/tde,tei->tdi/dot_general | solution.py:491
  154.2 1.9 %convolution_multiply_fusion = f32[8,64,128]{2,1,0:T(8,128)} fusion(f32[8,64,64]{2,1,0:T(8,128)} %get-tuple-element.12, bf16[8,64,1024]{2,1,0:T(8,128)(2,1)} %bitcast.9, s32[]{:T(128)S(6)} %select_n.11), kind=kOutput, calls=%fused_computation.9 | convolution fusion | flops 50397184 | bytes 655364 | tf_op jit(solution)/shard_map/tde,tei->tdi/dot_general | solution.py:490
  (3 shorter events, 0.0 us)
Async XLA Ops:
  1.3 74.4 %copy-start = (s32[8]{0:T(128)S(1)}, s32[8]{0:T(128)}, u32[]{:S(2)}) copy-start(s32[8]{0:T(128)} %param.21) | copy-start | bytes 100

commit v4 on v3

--- a/solution.py
+++ b/solution.py
@@ -28,23 +28,23 @@
     return hi, (x - hi.astype(F32)).astype(BF16)
 
 
-def probe_table(seeds, rank_size, order):
-    shape = (seeds.shape[0], rank_size, order)
-    chan = lax.broadcasted_iota(jnp.int32, shape, 1)
-    place = lax.broadcasted_iota(jnp.int32, shape, 2)
-    code = (
-        seeds[:, None, None] * 9973
+def probe_tile(seed, shape):
+    chan = lax.broadcasted_iota(jnp.int32, shape, 0)
+    place = lax.broadcasted_iota(jnp.int32, shape, 1)
+    code = lax.rem(
+        seed * 9973
         + place * place * 7
         + place * chan * 131
         + chan * chan * 17
         + place * 7919
-        + chan * 104729
-    ) % 65521
+        + chan * 104729,
+        jnp.full(shape, 65521, jnp.int32),
+    )
     return ((code.astype(F32) - 32760.0) / 32768.0).astype(BF16)
 
 
-def gather_kernel(nt, batch, low_right, near_right, count, u_ref, v_ref, low_v_ref, near_ref, *refs):
-    sv_ref, mix_ref, lh_ref, ll_ref, su, sv, low_v, near, send, recv, local, out_sem = refs
+def gather_kernel(nt, batch, low_right, near_right, count, seeds, u_ref, v_ref, low_v_ref, near_ref, *refs):
+    sv_ref, mix_ref, lh_ref, ll_ref, probe_ref, su, sv, low_v, near, send, recv, local, out_sem = refs
     me = lax.axis_index("tgt")
     k = u_ref.shape[0]
     h = k // 2
@@ -94,6 +94,21 @@
 
         lax.fori_loop(0, near.shape[0], body, 0)
 
+    def probes():
+        def body(t, carry):
+            probe_ref[t] = probe_tile(seeds[t], probe_ref.shape[1:])
+            return carry
+
+        lax.fori_loop(0, probe_ref.shape[0], body, 0)
+
+    outs = []
+
+    def emit(owner):
+        rows = pl.ds(owner * k, k)
+        c = pltpu.make_async_copy(sv.at[rows], sv_ref.at[rows], out_sem.at[len(outs)])
+        c.start()
+        outs.append(c)
+
     if nt == 4:
         a = me + 1 - 2 * (me % 2)
         b = (me + 2) % 4
@@ -119,6 +134,7 @@
             return [fa, push(dst.at[from_b], dst.at[from_b], sem + 1, a)]
 
         us = own(u_ref, su, 0)
+        probes()
         uf = onward(su, us, 4)
         vs = own(v_ref, sv, 6)
         for c in us[2:] + uf:
@@ -127,8 +143,14 @@
         mix()
         vf = onward(sv, vs, 10)
         lefts()
-        for c in vs[2:] + vf:
+        for c in vs[2:]:
             c.wait_recv()
+        loads[1].wait()
+        for owner in (me, a, b):
+            emit(owner)
+        for c in vf:
+            c.wait_recv()
+        emit(a + b - me)
         copies = us + uf + vs + vf
     else:
         for d in range(1, nt):
@@ -141,20 +163,22 @@
             to = (me + d) % nt
             copies.append(push(u_ref, su.at[mine], 2 * d - 2, to))
             copies.append(push(v_ref, sv.at[mine], 2 * d - 1, to))
+        probes()
         for c in copies:
             c.wait_recv()
         loads[0].wait()
         mix()
         lefts()
-    loads[1].wait()
-    out = pltpu.make_async_copy(sv, sv_ref, out_sem)
-    out.start()
+        loads[1].wait()
+        for d in range(nt):
+            emit((me + d) % nt)
     for c in copies:
         c.wait_send()
-    out.wait()
-
-
-def gather_tiles(nt, batch, low_right, near_right, count, u, v, low_v, near):
+    for c in outs:
+        c.wait()
+
+
+def gather_tiles(nt, batch, low_right, near_right, count, seeds, u, v, low_v, near):
     sems = 12 if nt == 4 else max(2 * nt - 2, 1)
     seg = (nt * u.shape[0],) + u.shape[1:]
     r = u.shape[1]
@@ -166,11 +190,12 @@
             jax.ShapeDtypeStruct((low_v.shape[0], low_v.shape[1], r), BF16),
             left,
             left,
+            jax.ShapeDtypeStruct((seeds.shape[0], r, near.shape[1]), BF16),
         ),
-        in_specs=[pl.BlockSpec(memory_space=pltpu.SMEM)] * 3
+        in_specs=[pl.BlockSpec(memory_space=pltpu.SMEM)] * 4
         + [pl.BlockSpec(memory_space=pl.ANY)] * 4,
         out_specs=[pl.BlockSpec(memory_space=pl.ANY)]
-        + [pl.BlockSpec(memory_space=pltpu.VMEM)] * 3,
+        + [pl.BlockSpec(memory_space=pltpu.VMEM)] * 4,
         scratch_shapes=[
             pltpu.VMEM(seg, u.dtype),
             pltpu.VMEM(seg, v.dtype),
@@ -179,12 +204,12 @@
             pltpu.SemaphoreType.DMA((sems,)),
             pltpu.SemaphoreType.DMA((sems,)),
             pltpu.SemaphoreType.DMA((4,)),
-            pltpu.SemaphoreType.DMA,
+            pltpu.SemaphoreType.DMA((nt,)),
         ],
         compiler_params=pltpu.CompilerParams(
             collective_id=0, has_side_effects=True, vmem_limit_bytes=VMEM_LIMIT
         ),
-    )(low_right, near_right, count, u, v, low_v, near)
+    )(low_right, near_right, count, seeds, u, v, low_v, near)
 
 
 def chol_inverse(s_ref, out_ref, a_ref):
@@ -446,10 +471,18 @@
     while lows // batch < slots:
         batch = batch // 2
     steps = lows // batch
-    seg_v, mixing, lh, ll = gather_tiles(
-        nt, batch, low_right, near_right, near_count, right_u, right_v, low_v, near_tiles
-    )
-    probe = probe_table(probe_seed, r, order)
+    seg_v, mixing, lh, ll, probe = gather_tiles(
+        nt,
+        batch,
+        low_right,
+        near_right,
+        near_count,
+        probe_seed,
+        right_u,
+        right_v,
+        low_v,
+        near_tiles,
+    )
     sk = jax.ShapeDtypeStruct((tiles, r, order), F32)
     near_specs = [at_near(seg_v.shape, slots)]
     pair_specs = (

time: 157 us -> 153 us (0.975)
  other arithmetic: 2.57 us -> 0 us
    convert_element_type x1 -> x0, other arithmetic: 2.56 us -> none  [probe_table(): return ((code.astype(F32) - 32760.0) / 32768.0).astype(BF16)]
where the time goes in v4:
time: 153 us
  Pallas kernels  147 us (96%)
  matrix products  4.05 us (3%)
    pallas_call x1, Pallas kernels, gather_tiles(): pl.pallas_call(functools.partial(gather_kernel, nt, batch), out_shape=(ja...  73.6 us
    pallas_call x2, Pallas kernels, reduce_inner(): pl.pallas_call(functools.partial(reduce_kernel, n, gather), out_shape=out...  53.1 us
    pallas_call x2, Pallas kernels, run(): pl.pallas_call(kernel, grid_spec=pltpu.PrefetchScalarGridSpec(num_scalar_...  20.5 us

profile of v4, /device:TPU:9, one launch (start us, length us, event | category | flops | bytes accessed | tf_op | source)
XLA Modules:
  0.0 152.7 jit_solution(3118089462476337895)
XLA Ops:
  1.3 73.6 %shard_map.122 = (bf16[32,64,1024]{2,1,0:T(8,128)(2,1)}, bf16[32,64,64]{2,1,0:T(8,128)(2,1)}, bf16[4,64,1024]{2,1,0:T(8,128)(2,1)}, bf16[4,64,1024]{2,1,0:T(8,128)(2,1)}, bf16[8,64,1024]{2,1,0:T(8,128)(2,1)}) custom-call(s32[32]{0:T(128)} %right.3, s32[4]{0:T(128)} %near_right.5, s32[1]{0:T(128)S(6)} %copy.13.count, s32[8]{0:T(128)} %seeds.1, ...), custom_call_target="tpu_custom_call" | custom-call | tf_op jit(solution)/shard_map/pallas_call | solution.py:186
  74.9 10.2 %shard_map.123 = f32[8,64,1024]{2,1,0:T(8,128)} custom-call(s32[32]{0:T(128)} %right.3, s32[32]{0:T(128)} %target.3, s32[4]{0:T(128)} %near_right.5, s32[4]{0:T(128)} %near_target.3, bf16[32,64,1024]{2,1,0:T(8,128)(2,1)} %get-tuple-element.9.refs_0_.refs_1_.refs_2_.refs_3_.refs_4_.refs_5_.refs_6_.refs_7_.refs_12_, ...), custom_call_target="tpu_custom_call" | custom-call | tf_op jit(solution)/shard_map/pallas_call | solution.py:441
  85.1 32.9 %shard_map.124 = bf16[4,2,64,1024]{3,2,1,0:T(8,128)(2,1)} custom-call(f32[4,2,64,1024]{3,2,1,0:T(8,128)} %bitcast.11), custom_call_target="tpu_custom_call" | custom-call | tf_op jit(solution)/shard_map/pallas_call | solution.py:329
  118.0 10.3 %shard_map.125 = f32[8,8,64,128]{3,2,1,0:T(8,128)} custom-call(s32[32]{0:T(128)} %right.3, s32[32]{0:T(128)} %target.3, s32[4]{0:T(128)} %near_right.5, s32[4]{0:T(128)} %near_target.3, bf16[32,64,1024]{2,1,0:T(8,128)(2,1)} %get-tuple-element.9.refs_0_.refs_1_.refs_2_.refs_3_.refs_4_.refs_5_.refs_6_.refs_7_.refs_12_, ...), custom_call_target="tpu_custom_call" | custom-call | tf_op jit(solution)/shard_map/pallas_call | solution.py:441
  128.4 20.2 %shard_map.126 = (f32[512,128]{1,0:T(8,128)}, f32[8,64,64]{2,1,0:T(8,128)}) custom-call(f32[4,2,512,128]{3,2,1,0:T(8,128)} %bitcast.10, bf16[8,64,1024]{2,1,0:T(8,128)(2,1)} %bitcast.8), custom_call_target="tpu_custom_call" | custom-call | tf_op jit(solution)/shard_map/pallas_call | solution.py:329
  148.6 2.1 %fusion.2 = f32[8,64,128]{2,1,0:T(8,128)} fusion(f32[8,64,64]{2,1,0:T(8,128)} %get-tuple-element.14, f32[8,64,128]{2,1,0:T(8,128)} %bitcast.12), kind=kOutput, calls=%fused_computation.3 | convolution fusion | flops 50331648 | bytes 655360 | tf_op jit(solution)/shard_map/tde,tei->tdi/dot_general | solution.py:524
  150.7 1.9 %convolution_multiply_fusion = f32[8,64,128]{2,1,0:T(8,128)} fusion(f32[8,64,64]{2,1,0:T(8,128)} %get-tuple-element.14, bf16[8,64,1024]{2,1,0:T(8,128)(2,1)} %bitcast.9, s32[]{:T(128)S(6)} %select_n.3), kind=kOutput, calls=%fused_computation | convolution fusion | flops 50397184 | bytes 655364 | tf_op jit(solution)/shard_map/tde,tei->tdi/dot_general | solution.py:523
